TPU v7x, 512 devices: a whole 4x8x8 slice. The times are simulated.
512 devices in a mesh: dp: 8 (over z_hi, core), latent: 64 (over z_lo, y, x).
Axes of the slice: x: 4, y: 8, z: 8 (z_hi: 4, z_lo: 2; z = z_hi * 2 + z_lo), core: 2. Of those that a mesh axis runs over, the one named last changes fastest.
Arguments:
- residual: bfloat16 [1536, 4608], P(('dp', 'latent')), may hold values from -6 to 6
- errors: bfloat16 [1536, 4608], P(('dp', 'latent')), may hold values from -192 to 192
- enc_weight: bfloat16 [4608, 8192], P(None, 'latent'), may hold values from -0.09375 to 0.09375
- dec_weight: bfloat16 [8192, 4608], P('latent'), may hold values from -0.09375 to 0.09375
- dead_mask: int32 [8192], P('latent'), may hold values from 0 to 1, as said below
Outputs:
- enc_grad: bfloat16 [4608, 8192], P(None, 'latent')
- dec_grad: bfloat16 [8192, 4608], P('latent')
Inputs may be any that keep to these rules, and one draw needn't show every extreme that they name: `dead_mask`: in each aligned block of 128 latents (the latents of one device) at most 64 are dead, and some block has exactly 64 dead latents.
All inputs are finite; a program needn't handle non-finite values.
Results may differ from a plain program's by a relative error of at most 0.017.
Values may be sent and summed in bfloat16 or wider, within the bound.
A program may use at most 64 MiB of HBM per device.

v0:
```python
import math

import jax
import jax.numpy as jnp
from jax import lax
from jax.sharding import PartitionSpec as P

eps_mean = 1e-06


def contract_rows(left_mat, right_mat):
    return lax.dot_general(
        left_mat, right_mat, (((0,), (0,)), ((), ())), preferred_element_type=jnp.float32
    )


def contract_cols(left_mat, right_mat):
    return lax.dot_general(
        left_mat, right_mat, (((1,), (1,)), ((), ())), preferred_element_type=jnp.float32
    )


def body(residual, errors, enc_weight, dec_weight, dead_mask):
    keep_mask = dead_mask.astype(jnp.float32)
    gathered = lax.all_gather(residual, "latent", axis=0, tiled=True)
    rows_all = gathered.shape[0]
    pre_acts = jnp.dot(gathered, enc_weight, preferred_element_type=jnp.float32)
    ghost_acts = jnp.exp(pre_acts) * keep_mask[None, :]
    acts_bf = ghost_acts.astype(jnp.bfloat16)
    acts_rows = acts_bf
    ghost_out = lax.psum_scatter(
        jnp.dot(acts_rows, dec_weight, preferred_element_type=jnp.float32),
        "latent",
        scatter_dimension=0,
        tiled=True,
    )
    err_full = errors.astype(jnp.float32)
    err_rms = jnp.sqrt(jnp.mean(err_full * err_full, axis=1, keepdims=True) + eps_mean)
    ghost_rms = jnp.sqrt(jnp.mean(ghost_out * ghost_out, axis=1, keepdims=True) + eps_mean)
    norm_scale = err_rms / (2.0 * ghost_rms)
    grad_out = (norm_scale * (norm_scale * ghost_out - err_full) / err_rms).astype(jnp.bfloat16)
    shard_piece = lax.all_gather(grad_out, "latent", axis=0, tiled=True)
    acts_rows = acts_bf
    dec_acc = contract_rows(acts_rows, shard_piece)
    back_grad = contract_cols(shard_piece, dec_weight)
    dec_acc, back_grad = (dec_acc, back_grad)
    pre_grad = (back_grad * ghost_acts).astype(jnp.bfloat16)
    enc_acc = contract_rows(gathered, pre_grad)
    factor = 1.0 / math.sqrt(rows_all * lax.axis_size("dp"))
    enc_sum, dec_sum = (
        lax.psum((enc_acc * factor).astype(jnp.bfloat16), "dp").astype(jnp.float32),
        lax.psum((dec_acc * factor).astype(jnp.bfloat16), "dp").astype(jnp.float32),
    )
    return (enc_sum.astype(jnp.bfloat16), dec_sum.astype(jnp.bfloat16))


def solution(mesh):
    placed = (
        P(("dp", "latent"), None),
        P(("dp", "latent"), None),
        P(None, "latent"),
        P("latent", None),
        P("latent"),
    )
    return jax.shard_map(
        body,
        mesh=mesh,
        in_specs=placed,
        out_specs=(P(None, "latent"), P("latent", None)),
        check_vma=False,
    )
```

profile of v0, /device:TPU:1, one launch (start us, length us, event | category | flops | bytes accessed | tf_op | source)
XLA Modules:
  0.0 1357.5 jit_solution(11940108703899207736)
XLA Ops:
  7.2 0.0 copy-start
  7.2 0.0 all-gather.5.cloned.1.call-start
  7.2 0.7 all-gather.5.cloned.1.call-update
  7.9 0.0 all-reduce.5.cloned.1.call-start
  8.0 0.7 convert_element_type.29
  8.6 266.4 %all-gather.5.cloned.1.call-done = bf16[64,3,4608]{2,1,0:T(4,128)(2,1)} async-done(((bf16[1,3,4608]{2,1,0:T(4,128)(2,1)}), bf16[64,3,4608]{2,1,0:T(4,128)(2,1)}) %all-gather.5.cloned.1.call-update) | async-done | bytes 1769488 | tf_op jit(solution)/shard_map/all_gather | solution.py:25
  275.0 3.3 reshape.28
  278.3 1.9 fusion.3
  280.2 0.0 copy-done
  280.2 2.4 fusion.11
  282.6 0.0 copy-start.2
  282.6 0.0 all-reduce.5.cloned.1.call-update
  282.6 0.0 all-gather.7.cloned.1.call-start
  282.7 1.3 dynamic-slice
  284.6 0.0 copy-done.2
  284.6 0.2 fusion.5
  284.8 614.8 %all-reduce.5.cloned.1.call-done = f32[192,4608]{1,0:T(8,128)} async-done(((f32[192,4608]{1,0:T(8,128)}), f32[192,4608]{1,0:T(8,128)}) %all-reduce.5.cloned.1.call-update) | async-done | bytes 3538960
  899.6 1.1 multiply_reduce_fusion
  900.7 1.7 fusion.9
  902.4 0.0 all-gather.7.cloned.1.call-update
  902.4 0.0 all-reduce.7.cloned.1.call-start
  902.5 298.8 %all-gather.7.cloned.1.call-done = bf16[64,3,4608]{2,1,0:T(4,128)(2,1)} async-done(((bf16[1,3,4608]{2,1,0:T(4,128)(2,1)}), bf16[64,3,4608]{2,1,0:T(4,128)(2,1)}) %all-gather.7.cloned.1.call-update) | async-done | bytes 1769488 | tf_op jit(solution)/shard_map/all_gather | solution.py:42
  1201.3 4.5 reshape.30
  1205.7 4.2 fusion.2
  1209.9 3.0 fusion.1
  1212.9 0.0 all-reduce.7.cloned.1.call-update
  1212.9 134.6 %all-reduce.7.cloned.1.call-done = (bf16[4608,128]{0,1:T(8,128)(2,1)}, bf16[128,4608]{1,0:T(8,128)(2,1)}) async-done(((bf16[4608,128]{0,1:T(8,128)(2,1)}, bf16[128,4608]{1,0:T(8,128)(2,1)}), (bf16[4608,128]{0,1:T(8,128)(2,1)}, bf16[128,4608]{1,0:T(8,128)(2,1)})) %all-reduce.7.cloned.1.call-update) | async-done | bytes 2359312 | tf_op jit(solution)/shard_map/psum | solution.py:51
  1347.5 0.0 copy-start.1
  1347.5 2.5 copy.9
  1349.9 0.0 copy-done.1
  1349.9 1.0 copy.13
  (1 shorter events, 0.0 us)
Async XLA Ops:
  7.2 273.0 %copy-start = (bf16[128,4608]{1,0:T(8,128)(2,1)S(1)}, bf16[128,4608]{1,0:T(8,128)(2,1)}, u32[]{:S(2)}) copy-start(bf16[128,4608]{1,0:T(8,128)(2,1)} %param.8) | copy-start | bytes 3538948
  7.2 267.8 %all-gather.5.cloned.1.call-start = ((), (), s32[]{:S(2)}) async-start(), calls=%async_computation | async-start | bytes 2396160 | tf_op jit(solution)/shard_map/all_gather | solution.py:25
  7.9 891.7 %all-reduce.5.cloned.1.call-start = ((), (), s32[]{:S(2)}) async-start(), calls=%async_computation.2 | async-start | bytes 7077888
  282.6 2.0 copy-start.2
  282.6 918.6 %all-gather.7.cloned.1.call-start = ((), (), s32[]{:S(2)}) async-start(), calls=%async_computation.1 | async-start | bytes 2396160 | tf_op jit(solution)/shard_map/all_gather | solution.py:42
  902.4 445.0 %all-reduce.7.cloned.1.call-start = ((), (), s32[]{:S(2)}) async-start(), calls=%async_computation.3 | async-start | bytes 4718592 | tf_op jit(solution)/shard_map/psum | solution.py:51
  1347.5 2.5 copy-start.1
Sparse Core Ops, SparseCore 0:
  10.1 264.8 all-gather.4
  282.7 616.7 all-reduce.4
  902.5 298.6 all-gather.6
  1213.0 134.3 all-reduce.6
where the time goes:
time: 1360 us
  waiting for transfers between devices  1320 us (97%)
  between operations  14.5 us (1%)
    unnamed x5, waiting for transfers between devices  616 us
    all_gather x1, waiting for transfers between devices, body(): shard_piece = lax.all_gather(grad_out, 'latent', axis=0, tiled=True)  299 us
    all_gather x1, waiting for transfers between devices, body(): gathered = lax.all_gather(residual, 'latent', axis=0, tiled=True)  266 us
    psum x1, waiting for transfers between devices, body(): lax.psum((enc_acc * factor).astype(jnp.bfloat16), 'dp').astype(jnp.float32)  135 us
  transfers between devices with their start and end apart: 4, of which 4 were waited for; matrix products, arithmetic and copies ran while one was open for 0% of the time, Pallas kernels for 0%

commit v1 on v0

v1 whole, which is shorter than its diff:
```python
import math

import jax
import jax.numpy as jnp
from jax import lax
from jax.experimental import pallas as pl
from jax.experimental.pallas import tpu as pltpu
from jax.sharding import PartitionSpec as P

NX, NY, NZ = 4, 8, 8
DEAD = 64
Q = 4
SLAB = 16
EPS = 1e-06
MESH = pl.DeviceIdType.MESH
F32, BF16 = jnp.float32, jnp.bfloat16


def dot_nt(a, b):
    return lax.dot_general(a, b, (((1,), (1,)), ((), ())), preferred_element_type=F32)


def dot_nn(a, b):
    return lax.dot_general(a, b, (((1,), (0,)), ((), ())), preferred_element_type=F32)


def dot_tn(a, b):
    return lax.dot_general(a, b, (((0,), (0,)), ((), ())), preferred_element_type=F32)


def iota(shape, dim):
    return lax.broadcasted_iota(jnp.int32, shape, dim)


def sum_quads(v):
    n = v.shape[0]
    row = iota(v.shape, 0)
    v = v + jnp.where(row % 2 == 0, pltpu.roll(v, n - 1, 0), pltpu.roll(v, 1, 0))
    return v + jnp.where(row % 4 < 2, pltpu.roll(v, n - 2, 0), pltpu.roll(v, 2, 0))


def fold(prod):
    same = iota(prod.shape, 0) % Q == iota(prod.shape, 1) // DEAD
    prod = jnp.where(same, prod, 0.0)
    half = 2 * DEAD
    pair = prod[:, :half] + prod[:, half:]
    return sum_quads(pair + pltpu.roll(pair, DEAD, 1))


def unfold(vals):
    wide = jnp.concatenate([vals, vals], axis=1)
    row = iota(wide.shape, 0)
    keep = (row % Q == iota(wide.shape, 1) // DEAD) & (row % SLAB < 3 * Q)
    return jnp.where(keep, wide, 0.0).astype(BF16)


def to_slab(ref, width):
    rows = iota((SLAB, width), 0)
    out = jnp.zeros((SLAB, width), F32)
    for r in range(3):
        for q in range(Q):
            piece = ref[r : r + 1, q * width : (q + 1) * width].astype(F32)
            out = jnp.where(rows == Q * r + q, piece, out)
    return out


def kernel(
    res_ref, err_ref, enc_ref, dec_ref, mask_ref,
    dgrad_ref, egrad_ref, pick_ref,
    e4, w4, rbuf, gbuf, obuf, osib, s1, xrecv, s2, yrecv, ghost, aexp, pexp, zsend, zrecv, zsum, zall,
    w_s, w_r, gy_s, gy_r, gx_s, gx_r, gs_s, gs_r, os_s, os_r, ox_s, ox_r, oy_s, oy_r,
    z_s, z_r, a_s, a_r, f_s, f_r,
):
    width = e4.shape[1]
    feats = width * Q
    plane = NX * NY
    dp, lat = lax.axis_index("dp"), lax.axis_index("latent")
    c, zhi = lax.rem(dp, 2), lax.div(dp, 2)
    zlo, inplane = lax.div(lat, plane), lax.rem(lat, plane)
    y, x = lax.div(inplane, NX), lax.rem(inplane, NX)
    z = zhi * 2 + zlo
    o = 1 - c
    own = zlo == c

    def at(xx, yy, zz, cc):
        return (lax.div(zz, 2) * 2 + cc, lax.rem(zz, 2) * plane + yy * NX + xx)

    def yof(d):
        return at(x, lax.rem(y + d, NY), z, c)

    def xof(d):
        return at(lax.rem(x + d, NX), y, z, c)

    def zof(d):
        return at(x, y, lax.rem(z + d, NZ), c)

    sibling = at(x, y, z, o)

    def remote(src, dst, send, recv, dev):
        return pltpu.make_async_remote_copy(
            src_ref=src, dst_ref=dst, send_sem=send, recv_sem=recv, device_id=dev, device_id_type=MESH
        )

    def block(cc, xx):
        return pl.ds((cc * NX + xx) * NY, NY)

    xorder = [d for d in (1, 3, 2) if d < NX]
    pending = []

    def go(copy):
        copy.start()
        pending.append(copy)
        return copy

    barrier = pltpu.get_barrier_semaphore()
    partners = [yof(d) for d in range(1, NY)] + [xof(d) for d in range(1, NX)] + [zof(d) for d in range(1, NZ)] + [sibling]
    for dev in partners:
        pl.semaphore_signal(barrier, inc=1, device_id=dev, device_id_type=MESH)
    pl.semaphore_wait(barrier, len(partners))

    def gather_y(buf, k):
        me = buf.at[pl.ds((c * NX + x) * NY + y, 1)]
        return [go(remote(me, me, gy_s.at[k, d - 1], gy_r.at[k, d - 1], yof(d))) for d in range(1, NY)]

    def gather_x(buf, k, ycopies):
        for copy in ycopies:
            copy.wait_recv()
        mine = buf.at[block(c, x)]
        xcopies = {d: go(remote(mine, mine, gx_s.at[k, d - 1], gx_r.at[k, d - 1], xof(d))) for d in xorder}
        forward = {0: go(remote(mine, mine, gs_s.at[k, 0], gs_r.at[k, 0], sibling))}
        return xcopies, forward

    def gather_next(buf, k, xcopies, forward, d):
        xcopies[d].wait_recv()
        got = buf.at[block(c, lax.rem(x + NX - d, NX))]
        forward[d] = go(remote(got, got, gs_s.at[k, d], gs_r.at[k, d], sibling))

    rbuf[pl.ds((c * NX + x) * NY + y, 1)] = to_slab(res_ref, width).astype(BF16)[None]
    ycopies = gather_y(rbuf, 0)

    mask = mask_ref[...].astype(F32)
    upper = (iota((128, 128), 0) <= iota((128, 128), 1)).astype(BF16)
    rank = dot_nn(jnp.broadcast_to(mask, (16, 128)).astype(BF16), upper)[0:1]
    slot = iota((DEAD, 128), 0).astype(F32) + 1.0
    pick = jnp.where((slot == rank) & (mask > 0.5), 1.0, 0.0).astype(BF16)
    pick_ref[...] = pick

    weights = [
        remote(ref, ref, w_s.at[i], w_r.at[i], at(x, y, z + 1 - 2 * zlo, c)) for i, ref in enumerate((e4, w4))
    ]

    @pl.when(own)
    def _():
        for q in range(Q):
            e4[pl.ds(q * DEAD, DEAD), :] = dot_nt(pick, enc_ref[q * width : (q + 1) * width, :]).astype(BF16)
        weights[0].start()
        for q in range(Q):
            w4[pl.ds(q * DEAD, DEAD), :] = dot_nn(pick, dec_ref[:, q * width : (q + 1) * width]).astype(BF16)
        weights[1].start()

    xcopies, forward = gather_x(rbuf, 0, ycopies)

    @pl.when(jnp.logical_not(own))
    def _():
        weights[0].wait_recv()
        weights[1].wait_recv()

    def run_block(cc, xx):
        rows = (NY * SLAB, width)
        here = pl.ds((cc * NX + xx) * NY * SLAB, NY * SLAB)
        pre = fold(dot_nt(rbuf[block(cc, xx)].reshape(rows), e4[...]))
        val = jnp.exp(pre)
        ghost[here, :] = val
        spread = unfold(val)
        aexp[here, :] = spread
        obuf[block(cc, xx)] = dot_nn(spread, w4[...]).astype(BF16).reshape(NY, SLAB, width)

    ocopies, oxcopies = {}, {}

    def add_sibling(d):
        xx = lax.rem(x + NX - d, NX)
        ocopies[d].wait_recv()
        s1[pl.ds(xx * NY, NY)] = (obuf[block(c, xx)].astype(F32) + osib[pl.ds(xx * NY, NY)].astype(F32)).astype(BF16)
        if d:
            t = NX - d
            oxcopies[t] = go(
                remote(s1.at[pl.ds(xx * NY, NY)], xrecv.at[pl.ds((t - 1) * NY, NY)], ox_s.at[t - 1], ox_r.at[t - 1], xof(t))
            )

    order = [0] + xorder
    for i, d in enumerate(order):
        xx = lax.rem(x + NX - d, NX)
        if d:
            gather_next(rbuf, 0, xcopies, forward, d)
        run_block(c, xx)
        forward[d].wait_recv()
        run_block(o, xx)
        ocopies[d] = go(remote(obuf.at[block(o, xx)], osib.at[pl.ds(xx * NY, NY)], os_s.at[d], os_r.at[d], sibling))
        if i > 1:
            add_sibling(order[i - 1])
    add_sibling(order[-1])
    add_sibling(0)

    for d in xorder:
        oxcopies[d].wait_recv()
    oycopies = []
    for d in list(range(1, NY)) + [0]:
        yy = lax.rem(y + d, NY)
        total = s1[pl.ds(x * NY + yy, 1)].astype(F32)
        for t in range(NX - 1):
            total += xrecv[pl.ds(t * NY + yy, 1)].astype(F32)
        if d:
            s2[pl.ds(d - 1, 1)] = total.astype(BF16)
            oycopies.append(
                go(remote(s2.at[pl.ds(d - 1, 1)], yrecv.at[pl.ds(d - 1, 1)], oy_s.at[d - 1], oy_r.at[d - 1], yof(d)))
            )
    out = total[0]
    for d in range(1, NY):
        oycopies[d - 1].wait_recv()
        out += yrecv[d - 1].astype(F32)

    def rms(v):
        squares = jnp.broadcast_to(jnp.sum(v * v, axis=1, keepdims=True), (SLAB, 128))
        return jnp.sqrt(sum_quads(squares) / feats + EPS)[:, 0:1]

    err = to_slab(err_ref, width)
    err_rms = rms(err)
    scale = err_rms / (2.0 * rms(out))
    gbuf[pl.ds((c * NX + x) * NY + y, 1)] = (scale * (scale * out - err) / err_rms).astype(BF16)[None]
    ycopies = gather_y(gbuf, 1)
    xcopies, forward = gather_x(gbuf, 1, ycopies)
    for d in xorder:
        gather_next(gbuf, 1, xcopies, forward, d)
    for d in order:
        forward[d].wait_recv()

    slots = 2 * Q // NZ
    tokens = 2 * plane * SLAB
    tile = min(width, 384)
    factor = 1.0 / math.sqrt(NZ * 2 * plane * 3)

    def gradient(lhs, rhs, base):
        left = lhs[...]
        for j in range(width // tile):
            cols = pl.ds(j * tile, tile)
            part = (dot_tn(left, rhs[:, :, cols].reshape(tokens, tile)) * factor).astype(BF16)
            for q in range(Q):
                zsend[base + q, :, cols] = part[q * DEAD : (q + 1) * DEAD]

    def send_z(first, last):
        for to in range(first // slots, last // slots):

            @pl.when(z != to)
            def _(to=to):
                remote(
                    zsend.at[pl.ds(to * slots, slots)], zrecv.at[z], z_s.at[to], z_r.at[z], at(x, y, to, c)
                ).start()

    gradient(aexp, gbuf, 0)
    send_z(0, Q)
    for b in range(2 * NX):
        here = pl.ds(b * NY * SLAB, NY * SLAB)
        back = fold(dot_nt(gbuf[pl.ds(b * NY, NY)].reshape(NY * SLAB, width), w4[...]))
        pexp[here, :] = unfold(back * ghost[here, :])
    gradient(pexp, rbuf, Q)
    send_z(Q, 2 * Q)

    zrecv[z] = zsend[pl.ds(z * slots, slots)]
    for to in range(NZ):

        @pl.when(z != to)
        def _(to=to):
            remote(
                zsend.at[pl.ds(to * slots, slots)], zrecv.at[to], z_s.at[to], z_r.at[to], at(x, y, to, c)
            ).wait()

    total = zrecv[0].astype(F32)
    for i in range(1, NZ):
        total += zrecv[i].astype(F32)
    zsum[...] = total.astype(BF16)

    def piece(i):
        return zall.at[pl.ds(i * slots, slots)]

    for j in range(NZ // 2):
        to = 2 * j + c

        @pl.when(z != to)
        def _(j=j, to=to):
            remote(zsum, piece(z), a_s.at[j], a_r.at[z], at(x, y, to, c)).start()

    def hand(d):
        i = lax.rem(z + d, NZ)
        return remote(piece(i), piece(i), f_s.at[d], f_r.at[d], sibling)

    @pl.when(own)
    def _():
        zall[pl.ds(z * slots, slots)] = zsum[...]
        for d in range(NZ):
            if d:
                i = lax.rem(z + d, NZ)
                remote(piece(i), piece(i), a_s.at[0], a_r.at[i], sibling).wait_recv()
            hand(d).start()

    @pl.when(jnp.logical_not(own))
    def _():
        for d in range(NZ):
            hand(d).wait_recv()

    for q in range(Q):
        dgrad_ref[:, q * width : (q + 1) * width] = zall[q]
        egrad_ref[:, q * width : (q + 1) * width] = zall[Q + q]

    for j in range(NZ // 2):

        @pl.when(z != 2 * j + c)
        def _(j=j):
            remote(zsum, piece(z), a_s.at[j], a_r.at[0], sibling).wait_send()

    @pl.when(own)
    def _():
        for copy in weights:
            copy.wait_send()
        for d in range(NZ):
            hand(d).wait_send()

    for copy in pending:
        copy.wait_send()


def body(residual, errors, enc_weight, dec_weight, dead_mask):
    feats = residual.shape[1]
    width = feats // Q
    slabs = 2 * NX * NY
    dma = pltpu.SemaphoreType.DMA
    vmem = pl.BlockSpec(memory_space=pltpu.VMEM)
    slots = 2 * Q // NZ
    lines = NX * NY

    def held(n):
        return pltpu.VMEM((n, SLAB, width), BF16)

    dgrad, egrad, pick = pl.pallas_call(
        kernel,
        out_shape=(
            jax.ShapeDtypeStruct((DEAD, feats), BF16),
            jax.ShapeDtypeStruct((DEAD, feats), BF16),
            jax.ShapeDtypeStruct((DEAD, 128), BF16),
        ),
        in_specs=[vmem] * 5,
        out_specs=(vmem,) * 3,
        scratch_shapes=[
            pltpu.VMEM((Q * DEAD, width), BF16),
            pltpu.VMEM((Q * DEAD, width), BF16),
            held(slabs),
            held(slabs),
            held(slabs),
            held(lines),
            held(lines),
            held(lines - NY),
            held(NY - 1),
            held(NY - 1),
            pltpu.VMEM((slabs * SLAB, 2 * DEAD), F32),
            pltpu.VMEM((slabs * SLAB, Q * DEAD), BF16),
            pltpu.VMEM((slabs * SLAB, Q * DEAD), BF16),
            pltpu.VMEM((2 * Q, DEAD, width), BF16),
            pltpu.VMEM((NZ, slots, DEAD, width), BF16),
            pltpu.VMEM((slots, DEAD, width), BF16),
            pltpu.VMEM((2 * Q, DEAD, width), BF16),
            dma((2,)), dma((2,)),
            dma((2, NY - 1)), dma((2, NY - 1)),
            dma((2, NX - 1)), dma((2, NX - 1)),
            dma((2, NX)), dma((2, NX)),
            dma((NX,)), dma((NX,)),
            dma((NX - 1,)), dma((NX - 1,)),
            dma((NY - 1,)), dma((NY - 1,)),
            dma((NZ,)), dma((NZ,)),
            dma((NZ // 2,)), dma((NZ,)),
            dma((NZ,)), dma((NZ,)),
        ],
        compiler_params=pltpu.CompilerParams(
            collective_id=0, has_side_effects=True, vmem_limit_bytes=48 * 1024 * 1024
        ),
    )(residual, errors, enc_weight, dec_weight, dead_mask.reshape(1, -1))
    enc_grad = dot_tn(egrad, pick).astype(BF16)
    dec_grad = dot_tn(pick, dgrad).astype(BF16)
    return enc_grad, dec_grad


def solution(mesh):
    return jax.shard_map(
        body,
        mesh=mesh,
        in_specs=(
            P(("dp", "latent"), None),
            P(("dp", "latent"), None),
            P(None, "latent"),
            P("latent", None),
            P("latent"),
        ),
        out_specs=(P(None, "latent"), P("latent", None)),
        check_vma=False,
    )
```

time: 1360 us -> 148 us (0.11)
  waiting for transfers between devices: 1320 us -> 0 us
  Pallas kernels: 0 us -> 137 us
  between operations: 14.5 us -> 0.65 us
    unnamed x5 -> x0, waiting for transfers between devices: 616 us -> none
    all_gather x2 -> x0, waiting for transfers between devices: 565 us -> none  [the longest x1 299 us: body(): shard_piece = lax.all_gather(grad_out, 'latent', axis=0, tiled=True)]
    pallas_call x0 -> x1, Pallas kernels: none -> 137 us  [body(): pl.pallas_call(kernel, out_shape=(jax.ShapeDtypeStruct((DEAD, feats), BF1...]
    psum x1 -> x0, waiting for transfers between devices: 135 us -> none  [body(): lax.psum((enc_acc * factor).astype(jnp.bfloat16), 'dp').astype(jnp.float32)]
  transfers between devices with their start and end apart: 4 -> 0, of which waited for: 4 -> 0; matrix products, arithmetic and copies ran while one was open for 0% -> 0% of each run, Pallas kernels for 0% -> 0%
where the time goes in v1:
time: 148 us; the launch traced here: 145 us
  Pallas kernels  137 us (93%)
  local copies, waits for them, and re-layouts  4.72 us (3%)
  matrix products  3.04 us (2%)
    pallas_call x1, Pallas kernels, body(): pl.pallas_call(kernel, out_shape=(jax.ShapeDtypeStruct((DEAD, feats), BF1...  137 us
    unnamed x10, local copies, waits for them, and re-layouts  4.72 us
    dot_general x2, matrix products, dot_tn(): lax.dot_general(a, b, (((0,), (0,)), ((), ())), preferred_element_type=F32)  3.04 us

profile of v1, /device:TPU:1, one launch (start us, length us, event | category | flops | bytes accessed | tf_op | source)
XLA Modules:
  0.0 145.1 jit_solution(5114543231124241489)
XLA Ops:
  0.6 0.0 copy-start
  0.6 1.3 copy-done
  1.9 0.0 copy-start.1
  1.9 1.3 copy-done.1
  3.2 0.0 copy-start.2
  3.2 0.8 copy-done.2
  3.9 0.0 copy-start.3
  3.9 0.8 copy-done.3
  4.7 0.0 copy-start.4
  4.7 0.7 copy-done.4
  5.4 136.7 %shard_map.68 = (bf16[64,4608]{1,0:T(8,128)(2,1)S(1)}, bf16[64,4608]{1,0:T(8,128)(2,1)S(1)}, bf16[64,128]{1,0:T(8,128)(2,1)S(1)}) custom-call(bf16[3,4608]{1,0:T(4,128)(2,1)S(1)} %copy-done.2, bf16[3,4608]{1,0:T(4,128)(2,1)S(1)} %copy-done.3, bf16[4608,128]{1,0:T(8,128)(2,1)S(1)} %copy-done, bf16[128,4608]{1,0:T(8,128)(2,1)S(1)} %copy-done.1, ...), custom_call_target="tpu_custom_call" | custom-call | tf_op jit(solution)/shard_map/pallas_call | solution.py:343
  142.0 1.5 %convolution_convert_fusion.1 = bf16[4608,128]{1,0:T(8,128)(2,1)} fusion(bf16[64,4608]{1,0:T(8,128)(2,1)S(1)} %get-tuple-element.5, bf16[64,128]{1,0:T(8,128)(2,1)S(1)} %get-tuple-element.6), kind=kOutput, calls=%fused_computation.1 | convolution fusion | flops 76087296 | bytes 1785856 | tf_op jit(solution)/shard_map/dot_general | solution.py:28
  143.6 1.5 %convolution_convert_fusion = bf16[128,4608]{1,0:T(8,128)(2,1)} fusion(bf16[64,128]{1,0:T(8,128)(2,1)S(1)} %get-tuple-element.6, bf16[64,4608]{1,0:T(8,128)(2,1)S(1)} %get-tuple-element.7), kind=kOutput, calls=%fused_computation | convolution fusion | flops 76087296 | bytes 1785856 | tf_op jit(solution)/shard_map/dot_general | solution.py:28
Async XLA Ops:
  0.6 1.3 copy-start
  1.9 1.3 copy-start.1
  3.2 0.8 copy-start.2
  3.9 0.8 copy-start.3
  4.7 0.7 copy-start.4

commit v2 on v1

--- a/solution.py
+++ b/solution.py
@@ -65,13 +65,22 @@
 
 
 def kernel(
-    res_ref, err_ref, enc_ref, dec_ref, mask_ref,
+    res_in, err_in, enc_in, dec_in, mask_in,
     dgrad_ref, egrad_ref, pick_ref,
-    e4, w4, rbuf, gbuf, obuf, osib, s1, xrecv, s2, yrecv, ghost, aexp, pexp, zsend, zrecv, zsum, zall,
+    e4, w4, rbuf, gbuf, obuf, osib, s1, xrecv, s2, yrecv, ghost, aexp, pexp, zsend, zhalf, zrecv, zall,
+    res_ref, err_ref, enc_ref, dec_ref, mask_ref, l_s,
     w_s, w_r, gy_s, gy_r, gx_s, gx_r, gs_s, gs_r, os_s, os_r, ox_s, ox_r, oy_s, oy_r,
-    z_s, z_r, a_s, a_r, f_s, f_r,
+    h_s, h_r, z_s, z_r, a_s, a_r, f_s, f_r,
 ):
     width = e4.shape[1]
+    loads = [
+        pltpu.make_async_copy(src, dst, l_s.at[i])
+        for i, (src, dst) in enumerate(
+            ((res_in, res_ref), (mask_in, mask_ref), (enc_in, enc_ref), (dec_in, dec_ref), (err_in, err_ref))
+        )
+    ]
+    for load in loads:
+        load.start()
     feats = width * Q
     plane = NX * NY
     dp, lat = lax.axis_index("dp"), lax.axis_index("latent")
@@ -118,26 +127,43 @@
         pl.semaphore_signal(barrier, inc=1, device_id=dev, device_id_type=MESH)
     pl.semaphore_wait(barrier, len(partners))
 
+    cut = width // 256 * 128 + (128 if width % 256 else 0) if width > 128 else 128
+    chunks = [pl.ds(0, cut)] + ([pl.ds(cut, width - cut)] if width > cut else [])
+
     def gather_y(buf, k):
-        me = buf.at[pl.ds((c * NX + x) * NY + y, 1)]
-        return [go(remote(me, me, gy_s.at[k, d - 1], gy_r.at[k, d - 1], yof(d))) for d in range(1, NY)]
+        me = (c * NX + x) * NY + y
+        copies = []
+        for h, cols in enumerate(chunks):
+            part = buf.at[pl.ds(me, 1), :, cols]
+            copies.append(
+                [go(remote(part, part, gy_s.at[k, h, d - 1], gy_r.at[k, h, d - 1], yof(d))) for d in range(1, NY)]
+            )
+        return copies
 
     def gather_x(buf, k, ycopies):
-        for copy in ycopies:
-            copy.wait_recv()
+        xcopies = []
+        for h, cols in enumerate(chunks):
+            for copy in ycopies[h]:
+                copy.wait_recv()
+            mine = buf.at[block(c, x), :, cols]
+            xcopies.append(
+                {d: go(remote(mine, mine, gx_s.at[k, h, d - 1], gx_r.at[k, h, d - 1], xof(d))) for d in xorder}
+            )
         mine = buf.at[block(c, x)]
-        xcopies = {d: go(remote(mine, mine, gx_s.at[k, d - 1], gx_r.at[k, d - 1], xof(d))) for d in xorder}
         forward = {0: go(remote(mine, mine, gs_s.at[k, 0], gs_r.at[k, 0], sibling))}
         return xcopies, forward
 
     def gather_next(buf, k, xcopies, forward, d):
-        xcopies[d].wait_recv()
+        for copies in xcopies:
+            copies[d].wait_recv()
         got = buf.at[block(c, lax.rem(x + NX - d, NX))]
         forward[d] = go(remote(got, got, gs_s.at[k, d], gs_r.at[k, d], sibling))
 
+    loads[0].wait()
     rbuf[pl.ds((c * NX + x) * NY + y, 1)] = to_slab(res_ref, width).astype(BF16)[None]
     ycopies = gather_y(rbuf, 0)
 
+    loads[1].wait()
     mask = mask_ref[...].astype(F32)
     upper = (iota((128, 128), 0) <= iota((128, 128), 1)).astype(BF16)
     rank = dot_nn(jnp.broadcast_to(mask, (16, 128)).astype(BF16), upper)[0:1]
@@ -148,6 +174,10 @@
     weights = [
         remote(ref, ref, w_s.at[i], w_r.at[i], at(x, y, z + 1 - 2 * zlo, c)) for i, ref in enumerate((e4, w4))
     ]
+
+    loads[2].wait()
+    loads[3].wait()
+    loads[4].wait()
 
     @pl.when(own)
     def _():
@@ -234,95 +264,126 @@
     for d in order:
         forward[d].wait_recv()
 
-    slots = 2 * Q // NZ
     tokens = 2 * plane * SLAB
     tile = min(width, 384)
     factor = 1.0 / math.sqrt(NZ * 2 * plane * 3)
-
-    def gradient(lhs, rhs, base):
+    owners = NZ // 2
+    slots = Q // owners
+    member = zhi
+    half = Q // 2
+
+    def gradient(lhs, rhs, kind):
         left = lhs[...]
         for j in range(width // tile):
             cols = pl.ds(j * tile, tile)
             part = (dot_tn(left, rhs[:, :, cols].reshape(tokens, tile)) * factor).astype(BF16)
             for q in range(Q):
-                zsend[base + q, :, cols] = part[q * DEAD : (q + 1) * DEAD]
-
-    def send_z(first, last):
-        for to in range(first // slots, last // slots):
-
-            @pl.when(z != to)
-            def _(to=to):
-                remote(
-                    zsend.at[pl.ds(to * slots, slots)], zrecv.at[z], z_s.at[to], z_r.at[z], at(x, y, to, c)
-                ).start()
+                zsend[kind * Q + q, :, cols] = part[q * DEAD : (q + 1) * DEAD]
+
+    def halves(kind):
+        return [
+            remote(
+                zsend.at[pl.ds(kind * Q + i * half, half)], zhalf.at[pl.ds(kind * Q + i * half, half)],
+                h_s.at[kind, i], h_r.at[kind, i], zof(d),
+            )
+            for i, d in enumerate((1, NZ - 1))
+        ]
+
+    def send_halves(kind):
+        @pl.when(jnp.logical_not(own))
+        def _():
+            for copy in halves(kind):
+                copy.start()
+
+    def to_member(kind, d):
+        m = lax.rem(member + d, owners)
+        return remote(
+            zsend.at[pl.ds(kind * Q + m * slots, slots)], zrecv.at[kind, d - 1],
+            z_s.at[kind, d - 1], z_r.at[kind, d - 1], zof(2 * d),
+        )
+
+    def spread_out(kind, d):
+        mine = zall.at[pl.ds(kind * Q + member * slots, slots)]
+        return remote(mine, mine, a_s.at[kind, d - 1], a_r.at[kind, d - 1], zof(2 * d))
+
+    def hand(kind, d):
+        piece = zall.at[pl.ds(kind * Q + lax.rem(member + owners - d, owners) * slots, slots)]
+        return remote(piece, piece, f_s.at[kind, d], f_r.at[kind, d], sibling)
+
+    others = [d for d in (1, 3, 2) if d < owners]
+
+    def add_halves(kind):
+        for copy in halves(kind):
+            copy.wait_recv()
+        for i in range(Q):
+            p = kind * Q + i
+            zsend[p] = (zsend[p].astype(F32) + zhalf[p].astype(F32)).astype(BF16)
+        for d in others:
+            to_member(kind, d).start()
+
+    def add_members(kind):
+        total = zsend[pl.ds(kind * Q + member * slots, slots)].astype(F32)
+        for d in others:
+            to_member(kind, d).wait_recv()
+            total += zrecv[kind, d - 1].astype(F32)
+        zall[pl.ds(kind * Q + member * slots, slots)] = total.astype(BF16)
+        for d in others:
+            spread_out(kind, d).start()
+        hand(kind, 0).start()
+
+    def hand_all(kind):
+        for d in others:
+            spread_out(kind, d).wait_recv()
+            hand(kind, d).start()
 
     gradient(aexp, gbuf, 0)
-    send_z(0, Q)
+    send_halves(0)
     for b in range(2 * NX):
         here = pl.ds(b * NY * SLAB, NY * SLAB)
         back = fold(dot_nt(gbuf[pl.ds(b * NY, NY)].reshape(NY * SLAB, width), w4[...]))
         pexp[here, :] = unfold(back * ghost[here, :])
-    gradient(pexp, rbuf, Q)
-    send_z(Q, 2 * Q)
-
-    zrecv[z] = zsend[pl.ds(z * slots, slots)]
-    for to in range(NZ):
-
-        @pl.when(z != to)
-        def _(to=to):
-            remote(
-                zsend.at[pl.ds(to * slots, slots)], zrecv.at[to], z_s.at[to], z_r.at[to], at(x, y, to, c)
-            ).wait()
-
-    total = zrecv[0].astype(F32)
-    for i in range(1, NZ):
-        total += zrecv[i].astype(F32)
-    zsum[...] = total.astype(BF16)
-
-    def piece(i):
-        return zall.at[pl.ds(i * slots, slots)]
-
-    for j in range(NZ // 2):
-        to = 2 * j + c
-
-        @pl.when(z != to)
-        def _(j=j, to=to):
-            remote(zsum, piece(z), a_s.at[j], a_r.at[z], at(x, y, to, c)).start()
-
-    def hand(d):
-        i = lax.rem(z + d, NZ)
-        return remote(piece(i), piece(i), f_s.at[d], f_r.at[d], sibling)
 
     @pl.when(own)
     def _():
-        zall[pl.ds(z * slots, slots)] = zsum[...]
-        for d in range(NZ):
-            if d:
-                i = lax.rem(z + d, NZ)
-                remote(piece(i), piece(i), a_s.at[0], a_r.at[i], sibling).wait_recv()
-            hand(d).start()
+        add_halves(0)
+
+    gradient(pexp, rbuf, 1)
+    send_halves(1)
+
+    @pl.when(own)
+    def _():
+        add_members(0)
+        add_halves(1)
+        hand_all(0)
+        add_members(1)
+        hand_all(1)
 
     @pl.when(jnp.logical_not(own))
     def _():
-        for d in range(NZ):
-            hand(d).wait_recv()
+        for kind in range(2):
+            for d in [0] + others:
+                hand(kind, d).wait_recv()
 
     for q in range(Q):
         dgrad_ref[:, q * width : (q + 1) * width] = zall[q]
         egrad_ref[:, q * width : (q + 1) * width] = zall[Q + q]
 
-    for j in range(NZ // 2):
-
-        @pl.when(z != 2 * j + c)
-        def _(j=j):
-            remote(zsum, piece(z), a_s.at[j], a_r.at[0], sibling).wait_send()
-
     @pl.when(own)
     def _():
         for copy in weights:
             copy.wait_send()
-        for d in range(NZ):
-            hand(d).wait_send()
+        for kind in range(2):
+            hand(kind, 0).wait_send()
+            for d in others:
+                to_member(kind, d).wait_send()
+                spread_out(kind, d).wait_send()
+                hand(kind, d).wait_send()
+
+    @pl.when(jnp.logical_not(own))
+    def _():
+        for kind in range(2):
+            for copy in halves(kind):
+                copy.wait_send()
 
     for copy in pending:
         copy.wait_send()
@@ -334,7 +395,7 @@
     slabs = 2 * NX * NY
     dma = pltpu.SemaphoreType.DMA
     vmem = pl.BlockSpec(memory_space=pltpu.VMEM)
-    slots = 2 * Q // NZ
+    owners = NZ // 2
     lines = NX * NY
 
     def held(n):
@@ -347,7 +408,7 @@
             jax.ShapeDtypeStruct((DEAD, feats), BF16),
             jax.ShapeDtypeStruct((DEAD, 128), BF16),
         ),
-        in_specs=[vmem] * 5,
+        in_specs=[pl.BlockSpec(memory_space=pl.ANY)] * 5,
         out_specs=(vmem,) * 3,
         scratch_shapes=[
             pltpu.VMEM((Q * DEAD, width), BF16),
@@ -364,22 +425,29 @@
             pltpu.VMEM((slabs * SLAB, Q * DEAD), BF16),
             pltpu.VMEM((slabs * SLAB, Q * DEAD), BF16),
             pltpu.VMEM((2 * Q, DEAD, width), BF16),
-            pltpu.VMEM((NZ, slots, DEAD, width), BF16),
-            pltpu.VMEM((slots, DEAD, width), BF16),
             pltpu.VMEM((2 * Q, DEAD, width), BF16),
+            pltpu.VMEM((2, max(owners - 1, 1), Q // owners, DEAD, width), BF16),
+            pltpu.VMEM((2 * Q, DEAD, width), BF16),
+            pltpu.VMEM(residual.shape, BF16),
+            pltpu.VMEM(errors.shape, BF16),
+            pltpu.VMEM(enc_weight.shape, BF16),
+            pltpu.VMEM(dec_weight.shape, BF16),
+            pltpu.VMEM((1, dead_mask.shape[0]), jnp.int32),
+            dma((5,)),
             dma((2,)), dma((2,)),
-            dma((2, NY - 1)), dma((2, NY - 1)),
-            dma((2, NX - 1)), dma((2, NX - 1)),
+            dma((2, 2, NY - 1)), dma((2, 2, NY - 1)),
+            dma((2, 2, NX - 1)), dma((2, 2, NX - 1)),
             dma((2, NX)), dma((2, NX)),
             dma((NX,)), dma((NX,)),
             dma((NX - 1,)), dma((NX - 1,)),
             dma((NY - 1,)), dma((NY - 1,)),
-            dma((NZ,)), dma((NZ,)),
-            dma((NZ // 2,)), dma((NZ,)),
-            dma((NZ,)), dma((NZ,)),
+            dma((2, 2)), dma((2, 2)),
+            dma((2, max(owners - 1, 1))), dma((2, max(owners - 1, 1))),
+            dma((2, max(owners - 1, 1))), dma((2, max(owners - 1, 1))),
+            dma((2, owners)), dma((2, owners)),
         ],
         compiler_params=pltpu.CompilerParams(
-            collective_id=0, has_side_effects=True, vmem_limit_bytes=48 * 1024 * 1024
+            collective_id=0, has_side_effects=True, vmem_limit_bytes=56 * 1024 * 1024
         ),
     )(residual, errors, enc_weight, dec_weight, dead_mask.reshape(1, -1))
     enc_grad = dot_tn(egrad, pick).astype(BF16)

time: 148 us -> 142 us (0.959); the launches traced: 145 us -> 142 us
  local copies, waits for them, and re-layouts: 4.72 us -> 0.01 us
    unnamed x10 -> x4, local copies, waits for them, and re-layouts: 4.72 us -> 0.01 us
where the time goes in v2:
time: 142 us
  Pallas kernels  137 us (96%)
  matrix products  4.16 us (3%)
    pallas_call x1, Pallas kernels, body(): pl.pallas_call(kernel, out_shape=(jax.ShapeDtypeStruct((DEAD, feats), BF1...  137 us
    dot_general x2, matrix products, dot_tn(): lax.dot_general(a, b, (((0,), (0,)), ((), ())), preferred_element_type=F32)  4.16 us

profile of v2, /device:TPU:1, one launch (start us, length us, event | category | flops | bytes accessed | tf_op | source)
XLA Modules:
  0.0 141.5 jit_solution(9257765488913812701)
XLA Ops:
  0.6 136.7 %shard_map.68 = (bf16[64,4608]{1,0:T(8,128)(2,1)}, bf16[64,4608]{1,0:T(8,128)(2,1)}, bf16[64,128]{1,0:T(8,128)(2,1)}) custom-call(bf16[3,4608]{1,0:T(4,128)(2,1)} %res_in.1, bf16[3,4608]{1,0:T(4,128)(2,1)} %err_in.1, bf16[4608,128]{1,0:T(8,128)(2,1)} %enc_in.1, bf16[128,4608]{1,0:T(8,128)(2,1)} %dec_in.1, s32[1,128]{1,0:T(1,128)} %bitcast.5), custom_call_target="tpu_custom_call" | custom-call | tf_op jit(solution)/shard_map/pallas_call | solution.py:404
  137.4 0.0 copy-start
  137.4 0.0 copy-start.1
  137.4 2.7 %convolution_convert_fusion.1 = bf16[4608,128]{1,0:T(8,128)(2,1)} fusion(bf16[64,4608]{1,0:T(8,128)(2,1)} %get-tuple-element.5, bf16[64,128]{1,0:T(8,128)(2,1)} %get-tuple-element.6), kind=kOutput, calls=%fused_computation.1 | convolution fusion | flops 76087296 | bytes 1785856 | tf_op jit(solution)/shard_map/dot_general | solution.py:28
  140.0 0.0 copy-done
  140.0 0.0 copy-done.1
  140.0 1.5 %convolution_convert_fusion = bf16[128,4608]{1,0:T(8,128)(2,1)} fusion(bf16[64,128]{1,0:T(8,128)(2,1)S(1)} %copy-done.1, bf16[64,4608]{1,0:T(8,128)(2,1)S(1)} %copy-done), kind=kOutput, calls=%fused_computation | convolution fusion | flops 76087296 | bytes 1785856 | tf_op jit(solution)/shard_map/dot_general | solution.py:28
Async XLA Ops:
  137.4 2.7 %copy-start = (bf16[64,4608]{1,0:T(8,128)(2,1)S(1)}, bf16[64,4608]{1,0:T(8,128)(2,1)}, u32[]{:S(2)}) copy-start(bf16[64,4608]{1,0:T(8,128)(2,1)} %get-tuple-element.7) | copy-start | bytes 1769476
  137.4 2.7 %copy-start.1 = (bf16[64,128]{1,0:T(8,128)(2,1)S(1)}, bf16[64,128]{1,0:T(8,128)(2,1)}, u32[]{:S(2)}) copy-start(bf16[64,128]{1,0:T(8,128)(2,1)} %get-tuple-element.6) | copy-start | bytes 49156

commit v3 on v2

--- a/solution.py
+++ b/solution.py
@@ -67,7 +67,7 @@
 def kernel(
     res_in, err_in, enc_in, dec_in, mask_in,
     dgrad_ref, egrad_ref, pick_ref,
-    e4, w4, rbuf, gbuf, obuf, osib, s1, xrecv, s2, yrecv, ghost, aexp, pexp, zsend, zhalf, zrecv, zall,
+    e4, w4, rbuf, gbuf, obuf, osib, s1, xrecv, s2, yrecv, ghost, aexp, pexp, zsend, zhalf, zrel, zrecv, zall,
     res_ref, err_ref, enc_ref, dec_ref, mask_ref, l_s,
     w_s, w_r, gy_s, gy_r, gx_s, gx_r, gs_s, gs_r, os_s, os_r, ox_s, ox_r, oy_s, oy_r,
     h_s, h_r, z_s, z_r, a_s, a_r, f_s, f_r,
@@ -122,7 +122,7 @@
         return copy
 
     barrier = pltpu.get_barrier_semaphore()
-    partners = [yof(d) for d in range(1, NY)] + [xof(d) for d in range(1, NX)] + [zof(d) for d in range(1, NZ)] + [sibling]
+    partners = [yof(d) for d in range(1, NY)] + [xof(d) for d in range(1, NX)] + [zof(d) for d in (1, 2, NZ - 2, NZ - 1)] + [sibling]
     for dev in partners:
         pl.semaphore_signal(barrier, inc=1, device_id=dev, device_id_type=MESH)
     pl.semaphore_wait(barrier, len(partners))
@@ -267,9 +267,11 @@
     tokens = 2 * plane * SLAB
     tile = min(width, 384)
     factor = 1.0 / math.sqrt(NZ * 2 * plane * 3)
-    owners = NZ // 2
-    slots = Q // owners
-    member = zhi
+    to_left = lax.rem(zhi + Q - 1, Q)
+    to_right = lax.rem(zhi + 1, Q)
+    across = lax.rem(zhi + 2, Q)
+    right, left = zof(2), zof(NZ - 2)
+    top, low = pl.ds(0, DEAD // 2), pl.ds(DEAD // 2, DEAD // 2)
     half = Q // 2
 
     def gradient(lhs, rhs, kind):
@@ -295,46 +297,69 @@
             for copy in halves(kind):
                 copy.start()
 
-    def to_member(kind, d):
-        m = lax.rem(member + d, owners)
-        return remote(
-            zsend.at[pl.ds(kind * Q + m * slots, slots)], zrecv.at[kind, d - 1],
-            z_s.at[kind, d - 1], z_r.at[kind, d - 1], zof(2 * d),
+    def z_copy(kind, i):
+        k = kind * Q
+        pairs = (
+            (zsend.at[k + across, top], zrel.at[kind, 0], right),
+            (zsend.at[k + across, low], zrel.at[kind, 1], left),
+            (zsend.at[k + to_right, low], zrecv.at[kind, 0, low], right),
+            (zsend.at[k + to_left, top], zrecv.at[kind, 1, top], left),
+            (zsend.at[k + to_right, top], zrecv.at[kind, 0, top], right),
+            (zsend.at[k + to_left, low], zrecv.at[kind, 1, low], left),
         )
-
-    def spread_out(kind, d):
-        mine = zall.at[pl.ds(kind * Q + member * slots, slots)]
-        return remote(mine, mine, a_s.at[kind, d - 1], a_r.at[kind, d - 1], zof(2 * d))
-
-    def hand(kind, d):
-        piece = zall.at[pl.ds(kind * Q + lax.rem(member + owners - d, owners) * slots, slots)]
-        return remote(piece, piece, f_s.at[kind, d], f_r.at[kind, d], sibling)
-
-    others = [d for d in (1, 3, 2) if d < owners]
+        src, dst, dev = pairs[i]
+        return remote(src, dst, z_s.at[kind, i], z_r.at[kind, i], dev)
+
+    def a_copy(kind, i):
+        sent = (
+            (zhi, top, right), (zhi, low, left), (zhi, low, right), (zhi, top, left),
+            (to_left, top, right), (to_right, low, left),
+        )
+        p, rows, dev = sent[i]
+        part = zall.at[kind * Q + p, rows]
+        return remote(part, part, a_s.at[kind, i], a_r.at[kind, i], dev)
+
+    def hand(kind, i):
+        piece = zall.at[kind * Q + (zhi, to_left, to_right, across)[i]]
+        return remote(piece, piece, f_s.at[kind, i], f_r.at[kind, i], sibling)
 
     def add_halves(kind):
         for copy in halves(kind):
             copy.wait_recv()
-        for i in range(Q):
-            p = kind * Q + i
+        for p, sends in ((across, (0, 1)), (to_right, (2,)), (to_left, (3,)), (zhi, ())):
+            p = kind * Q + p
             zsend[p] = (zsend[p].astype(F32) + zhalf[p].astype(F32)).astype(BF16)
-        for d in others:
-            to_member(kind, d).start()
+            for i in sends:
+                z_copy(kind, i).start()
+
+    def relay(kind):
+        for i, p, rows in ((0, to_right, top), (1, to_left, low)):
+            z_copy(kind, i).wait_recv()
+            p = kind * Q + p
+            zsend[p, rows] = (zsend[p, rows].astype(F32) + zrel[kind, i].astype(F32)).astype(BF16)
+            z_copy(kind, 4 + i).start()
 
     def add_members(kind):
-        total = zsend[pl.ds(kind * Q + member * slots, slots)].astype(F32)
-        for d in others:
-            to_member(kind, d).wait_recv()
-            total += zrecv[kind, d - 1].astype(F32)
-        zall[pl.ds(kind * Q + member * slots, slots)] = total.astype(BF16)
-        for d in others:
-            spread_out(kind, d).start()
+        for i in range(2, 6):
+            z_copy(kind, i).wait_recv()
+        p = kind * Q + zhi
+        zall[p] = (zsend[p].astype(F32) + zrecv[kind, 0].astype(F32) + zrecv[kind, 1].astype(F32)).astype(BF16)
+        for i in range(4):
+            a_copy(kind, i).start()
         hand(kind, 0).start()
 
-    def hand_all(kind):
-        for d in others:
-            spread_out(kind, d).wait_recv()
-            hand(kind, d).start()
+    def share(kind):
+        for i in range(2):
+            a_copy(kind, i).wait_recv()
+            a_copy(kind, 4 + i).start()
+        for i in range(2):
+            a_copy(kind, 2 + i).wait_recv()
+            hand(kind, 1 + i).start()
+
+    def finish(kind):
+        for i in range(4, 6):
+            a_copy(kind, i).wait_recv()
+        hand(kind, 3).start()
 
     gradient(aexp, gbuf, 0)
     send_halves(0)
@@ -352,17 +377,21 @@
 
     @pl.when(own)
     def _():
+        relay(0)
+        add_halves(1)
         add_members(0)
-        add_halves(1)
-        hand_all(0)
+        relay(1)
+        share(0)
         add_members(1)
-        hand_all(1)
+        finish(0)
+        share(1)
+        finish(1)
 
     @pl.when(jnp.logical_not(own))
     def _():
         for kind in range(2):
-            for d in [0] + others:
-                hand(kind, d).wait_recv()
+            for i in range(Q):
+                hand(kind, i).wait_recv()
 
     for q in range(Q):
         dgrad_ref[:, q * width : (q + 1) * width] = zall[q]
@@ -373,11 +402,11 @@
         for copy in weights:
             copy.wait_send()
         for kind in range(2):
-            hand(kind, 0).wait_send()
-            for d in others:
-                to_member(kind, d).wait_send()
-                spread_out(kind, d).wait_send()
-                hand(kind, d).wait_send()
+            for i in range(6):
+                z_copy(kind, i).wait_send()
+                a_copy(kind, i).wait_send()
+            for i in range(Q):
+                hand(kind, i).wait_send()
 
     @pl.when(jnp.logical_not(own))
     def _():
@@ -395,7 +424,6 @@
     slabs = 2 * NX * NY
     dma = pltpu.SemaphoreType.DMA
     vmem = pl.BlockSpec(memory_space=pltpu.VMEM)
-    owners = NZ // 2
     lines = NX * NY
 
     def held(n):
@@ -426,7 +454,8 @@
             pltpu.VMEM((slabs * SLAB, Q * DEAD), BF16),
             pltpu.VMEM((2 * Q, DEAD, width), BF16),
             pltpu.VMEM((2 * Q, DEAD, width), BF16),
-            pltpu.VMEM((2, max(owners - 1, 1), Q // owners, DEAD, width), BF16),
+            pltpu.VMEM((2, 2, DEAD // 2, width), BF16),
+            pltpu.VMEM((2, 2, DEAD, width), BF16),
             pltpu.VMEM((2 * Q, DEAD, width), BF16),
             pltpu.VMEM(residual.shape, BF16),
             pltpu.VMEM(errors.shape, BF16),
@@ -442,9 +471,9 @@
             dma((NX - 1,)), dma((NX - 1,)),
             dma((NY - 1,)), dma((NY - 1,)),
             dma((2, 2)), dma((2, 2)),
-            dma((2, max(owners - 1, 1))), dma((2, max(owners - 1, 1))),
-            dma((2, max(owners - 1, 1))), dma((2, max(owners - 1, 1))),
-            dma((2, owners)), dma((2, owners)),
+            dma((2, 6)), dma((2, 6)),
+            dma((2, 6)), dma((2, 6)),
+            dma((2, Q)), dma((2, Q)),
         ],
         compiler_params=pltpu.CompilerParams(
             collective_id=0, has_side_effects=True, vmem_limit_bytes=56 * 1024 * 1024

time: 142 us -> 133 us (0.937)
  Pallas kernels: 137 us -> 128 us
    pallas_call x1, Pallas kernels: 137 us -> 128 us  [body(): pl.pallas_call(kernel, out_shape=(jax.ShapeDtypeStruct((DEAD, feats), BF1...]
where the time goes in v3:
time: 133 us
  Pallas kernels  128 us (96%)
  matrix products  4.16 us (3%)
    pallas_call x1, Pallas kernels, body(): pl.pallas_call(kernel, out_shape=(jax.ShapeDtypeStruct((DEAD, feats), BF1...  128 us
    dot_general x2, matrix products, dot_tn(): lax.dot_general(a, b, (((0,), (0,)), ((), ())), preferred_element_type=F32)  4.16 us

profile of v3, /device:TPU:1, one launch (start us, length us, event | category | flops | bytes accessed | tf_op | source)
XLA Modules:
  0.0 133.2 jit_solution(12309616779993176039)
XLA Ops:
  0.6 128.4 %shard_map.68 = (bf16[64,4608]{1,0:T(8,128)(2,1)}, bf16[64,4608]{1,0:T(8,128)(2,1)}, bf16[64,128]{1,0:T(8,128)(2,1)}) custom-call(bf16[3,4608]{1,0:T(4,128)(2,1)} %res_in.1, bf16[3,4608]{1,0:T(4,128)(2,1)} %err_in.1, bf16[4608,128]{1,0:T(8,128)(2,1)} %enc_in.1, bf16[128,4608]{1,0:T(8,128)(2,1)} %dec_in.1, s32[1,128]{1,0:T(1,128)} %bitcast.5), custom_call_target="tpu_custom_call" | custom-call | tf_op jit(solution)/shard_map/pallas_call | solution.py:432
  129.0 0.0 copy-start
  129.0 0.0 copy-start.1
  129.1 2.7 %convolution_convert_fusion.1 = bf16[4608,128]{1,0:T(8,128)(2,1)} fusion(bf16[64,4608]{1,0:T(8,128)(2,1)} %get-tuple-element.5, bf16[64,128]{1,0:T(8,128)(2,1)} %get-tuple-element.6), kind=kOutput, calls=%fused_computation.1 | convolution fusion | flops 76087296 | bytes 1785856 | tf_op jit(solution)/shard_map/dot_general | solution.py:28
  131.7 0.0 copy-done
  131.7 0.0 copy-done.1
  131.7 1.5 %convolution_convert_fusion = bf16[128,4608]{1,0:T(8,128)(2,1)} fusion(bf16[64,128]{1,0:T(8,128)(2,1)S(1)} %copy-done.1, bf16[64,4608]{1,0:T(8,128)(2,1)S(1)} %copy-done), kind=kOutput, calls=%fused_computation | convolution fusion | flops 76087296 | bytes 1785856 | tf_op jit(solution)/shard_map/dot_general | solution.py:28
Async XLA Ops:
  129.0 2.7 %copy-start = (bf16[64,4608]{1,0:T(8,128)(2,1)S(1)}, bf16[64,4608]{1,0:T(8,128)(2,1)}, u32[]{:S(2)}) copy-start(bf16[64,4608]{1,0:T(8,128)(2,1)} %get-tuple-element.7) | copy-start | bytes 1769476
  129.0 2.7 %copy-start.1 = (bf16[64,128]{1,0:T(8,128)(2,1)S(1)}, bf16[64,128]{1,0:T(8,128)(2,1)}, u32[]{:S(2)}) copy-start(bf16[64,128]{1,0:T(8,128)(2,1)} %get-tuple-element.6) | copy-start | bytes 49156

commit v4 on v3

--- a/solution.py
+++ b/solution.py
@@ -11,6 +11,7 @@
 DEAD = 64
 Q = 4
 SLAB = 16
+REAL = 3 * Q
 EPS = 1e-06
 MESH = pl.DeviceIdType.MESH
 F32, BF16 = jnp.float32, jnp.bfloat16
@@ -50,8 +51,7 @@
 def unfold(vals):
     wide = jnp.concatenate([vals, vals], axis=1)
     row = iota(wide.shape, 0)
-    keep = (row % Q == iota(wide.shape, 1) // DEAD) & (row % SLAB < 3 * Q)
-    return jnp.where(keep, wide, 0.0).astype(BF16)
+    return jnp.where(row % Q == iota(wide.shape, 1) // DEAD, wide, 0.0).astype(BF16)
 
 
 def to_slab(ref, width):
@@ -67,7 +67,7 @@
 def kernel(
     res_in, err_in, enc_in, dec_in, mask_in,
     dgrad_ref, egrad_ref, pick_ref,
-    e4, w4, rbuf, gbuf, obuf, osib, s1, xrecv, s2, yrecv, ghost, aexp, pexp, zsend, zhalf, zrel, zrecv, zall,
+    e4, w4, ybuf, rbuf, gbuf, obuf, osib, s1, xrecv, s2, yrecv, ghost, aexp, pexp, zsend, zhalf, zrel, zrecv, zall,
     res_ref, err_ref, enc_ref, dec_ref, mask_ref, l_s,
     w_s, w_r, gy_s, gy_r, gx_s, gx_r, gs_s, gs_r, os_s, os_r, ox_s, ox_r, oy_s, oy_r,
     h_s, h_r, z_s, z_r, a_s, a_r, f_s, f_r,
@@ -111,7 +111,7 @@
         )
 
     def block(cc, xx):
-        return pl.ds((cc * NX + xx) * NY, NY)
+        return pl.ds(cc * NX + xx, 1)
 
     xorder = [d for d in (1, 3, 2) if d < NX]
     pending = []
@@ -130,11 +130,14 @@
     cut = width // 256 * 128 + (128 if width % 256 else 0) if width > 128 else 128
     chunks = [pl.ds(0, cut)] + ([pl.ds(cut, width - cut)] if width > cut else [])
 
-    def gather_y(buf, k):
-        me = (c * NX + x) * NY + y
+    line = NY * REAL
+    slot, place = iota((line, NY * SLAB), 0), iota((line, NY * SLAB), 1)
+    pack = jnp.where(slot // REAL * SLAB + slot % REAL == place, 1.0, 0.0).astype(BF16)
+
+    def gather_y(k):
         copies = []
         for h, cols in enumerate(chunks):
-            part = buf.at[pl.ds(me, 1), :, cols]
+            part = ybuf.at[k, pl.ds(y, 1), :, cols]
             copies.append(
                 [go(remote(part, part, gy_s.at[k, h, d - 1], gy_r.at[k, h, d - 1], yof(d))) for d in range(1, NY)]
             )
@@ -145,6 +148,8 @@
         for h, cols in enumerate(chunks):
             for copy in ycopies[h]:
                 copy.wait_recv()
+            slabs = ybuf[k, :, :, cols].reshape(NY * SLAB, -1)
+            buf[block(c, x), :, cols] = dot_nn(pack, slabs).astype(BF16)[None]
             mine = buf.at[block(c, x), :, cols]
             xcopies.append(
                 {d: go(remote(mine, mine, gx_s.at[k, h, d - 1], gx_r.at[k, h, d - 1], xof(d))) for d in xorder}
@@ -160,15 +165,15 @@
         forward[d] = go(remote(got, got, gs_s.at[k, d], gs_r.at[k, d], sibling))
 
     loads[0].wait()
-    rbuf[pl.ds((c * NX + x) * NY + y, 1)] = to_slab(res_ref, width).astype(BF16)[None]
-    ycopies = gather_y(rbuf, 0)
+    ybuf[0, pl.ds(y, 1)] = to_slab(res_ref, width).astype(BF16)[None]
+    ycopies = gather_y(0)
 
     loads[1].wait()
     mask = mask_ref[...].astype(F32)
     upper = (iota((128, 128), 0) <= iota((128, 128), 1)).astype(BF16)
     rank = dot_nn(jnp.broadcast_to(mask, (16, 128)).astype(BF16), upper)[0:1]
-    slot = iota((DEAD, 128), 0).astype(F32) + 1.0
-    pick = jnp.where((slot == rank) & (mask > 0.5), 1.0, 0.0).astype(BF16)
+    order = iota((DEAD, 128), 0).astype(F32) + 1.0
+    pick = jnp.where((order == rank) & (mask > 0.5), 1.0, 0.0).astype(BF16)
     pick_ref[...] = pick
 
     weights = [
@@ -196,25 +201,25 @@
         weights[1].wait_recv()
 
     def run_block(cc, xx):
-        rows = (NY * SLAB, width)
-        here = pl.ds((cc * NX + xx) * NY * SLAB, NY * SLAB)
-        pre = fold(dot_nt(rbuf[block(cc, xx)].reshape(rows), e4[...]))
+        b = cc * NX + xx
+        here = pl.ds(pl.multiple_of(b * line, 32 if line % 32 == 0 else 8), line)
+        pre = fold(dot_nt(rbuf[b], e4[...]))
         val = jnp.exp(pre)
         ghost[here, :] = val
         spread = unfold(val)
         aexp[here, :] = spread
-        obuf[block(cc, xx)] = dot_nn(spread, w4[...]).astype(BF16).reshape(NY, SLAB, width)
+        obuf[b] = dot_nn(spread, w4[...]).astype(BF16)
 
     ocopies, oxcopies = {}, {}
 
     def add_sibling(d):
         xx = lax.rem(x + NX - d, NX)
         ocopies[d].wait_recv()
-        s1[pl.ds(xx * NY, NY)] = (obuf[block(c, xx)].astype(F32) + osib[pl.ds(xx * NY, NY)].astype(F32)).astype(BF16)
+        s1[xx] = (obuf[c * NX + xx].astype(F32) + osib[xx].astype(F32)).astype(BF16)
         if d:
             t = NX - d
             oxcopies[t] = go(
-                remote(s1.at[pl.ds(xx * NY, NY)], xrecv.at[pl.ds((t - 1) * NY, NY)], ox_s.at[t - 1], ox_r.at[t - 1], xof(t))
+                remote(s1.at[xx], xrecv.at[t - 1], ox_s.at[t - 1], ox_r.at[t - 1], xof(t))
             )
 
     order = [0] + xorder
@@ -225,7 +230,7 @@
         run_block(c, xx)
         forward[d].wait_recv()
         run_block(o, xx)
-        ocopies[d] = go(remote(obuf.at[block(o, xx)], osib.at[pl.ds(xx * NY, NY)], os_s.at[d], os_r.at[d], sibling))
+        ocopies[d] = go(remote(obuf.at[o * NX + xx], osib.at[xx], os_s.at[d], os_r.at[d], sibling))
         if i > 1:
             add_sibling(order[i - 1])
     add_sibling(order[-1])
@@ -233,18 +238,16 @@
 
     for d in xorder:
         oxcopies[d].wait_recv()
+    total = s1[x].astype(F32)
+    for t in range(NX - 1):
+        total += xrecv[t].astype(F32)
+    s2[...] = dot_tn(pack, total.astype(BF16)).astype(BF16).reshape(NY, SLAB, width)
     oycopies = []
-    for d in list(range(1, NY)) + [0]:
-        yy = lax.rem(y + d, NY)
-        total = s1[pl.ds(x * NY + yy, 1)].astype(F32)
-        for t in range(NX - 1):
-            total += xrecv[pl.ds(t * NY + yy, 1)].astype(F32)
-        if d:
-            s2[pl.ds(d - 1, 1)] = total.astype(BF16)
-            oycopies.append(
-                go(remote(s2.at[pl.ds(d - 1, 1)], yrecv.at[pl.ds(d - 1, 1)], oy_s.at[d - 1], oy_r.at[d - 1], yof(d)))
-            )
-    out = total[0]
+    for d in range(1, NY):
+        oycopies.append(
+            go(remote(s2.at[lax.rem(y + d, NY)], yrecv.at[d - 1], oy_s.at[d - 1], oy_r.at[d - 1], yof(d)))
+        )
+    out = s2[y].astype(F32)
     for d in range(1, NY):
         oycopies[d - 1].wait_recv()
         out += yrecv[d - 1].astype(F32)
@@ -256,15 +259,15 @@
     err = to_slab(err_ref, width)
     err_rms = rms(err)
     scale = err_rms / (2.0 * rms(out))
-    gbuf[pl.ds((c * NX + x) * NY + y, 1)] = (scale * (scale * out - err) / err_rms).astype(BF16)[None]
-    ycopies = gather_y(gbuf, 1)
+    ybuf[1, pl.ds(y, 1)] = (scale * (scale * out - err) / err_rms).astype(BF16)[None]
+    ycopies = gather_y(1)
     xcopies, forward = gather_x(gbuf, 1, ycopies)
     for d in xorder:
         gather_next(gbuf, 1, xcopies, forward, d)
     for d in order:
         forward[d].wait_recv()
 
-    tokens = 2 * plane * SLAB
+    tokens = 2 * plane * REAL
     tile = min(width, 384)
     factor = 1.0 / math.sqrt(NZ * 2 * plane * 3)
     to_left = lax.rem(zhi + Q - 1, Q)
@@ -364,8 +367,8 @@
     gradient(aexp, gbuf, 0)
     send_halves(0)
     for b in range(2 * NX):
-        here = pl.ds(b * NY * SLAB, NY * SLAB)
-        back = fold(dot_nt(gbuf[pl.ds(b * NY, NY)].reshape(NY * SLAB, width), w4[...]))
+        here = pl.ds(b * line, line)
+        back = fold(dot_nt(gbuf[b], w4[...]))
         pexp[here, :] = unfold(back * ghost[here, :])
 
     @pl.when(own)
@@ -421,13 +424,12 @@
 def body(residual, errors, enc_weight, dec_weight, dead_mask):
     feats = residual.shape[1]
     width = feats // Q
-    slabs = 2 * NX * NY
+    line = NY * REAL
     dma = pltpu.SemaphoreType.DMA
     vmem = pl.BlockSpec(memory_space=pltpu.VMEM)
-    lines = NX * NY
 
     def held(n):
-        return pltpu.VMEM((n, SLAB, width), BF16)
+        return pltpu.VMEM((n, line, width), BF16)
 
     dgrad, egrad, pick = pl.pallas_call(
         kernel,
@@ -441,17 +443,18 @@
         scratch_shapes=[
             pltpu.VMEM((Q * DEAD, width), BF16),
             pltpu.VMEM((Q * DEAD, width), BF16),
-            held(slabs),
-            held(slabs),
-            held(slabs),
-            held(lines),
-            held(lines),
-            held(lines - NY),
-            held(NY - 1),
-            held(NY - 1),
-            pltpu.VMEM((slabs * SLAB, 2 * DEAD), F32),
-            pltpu.VMEM((slabs * SLAB, Q * DEAD), BF16),
-            pltpu.VMEM((slabs * SLAB, Q * DEAD), BF16),
+            pltpu.VMEM((2, NY, SLAB, width), BF16),
+            held(2 * NX),
+            held(2 * NX),
+            held(2 * NX),
+            held(NX),
+            held(NX),
+            held(NX - 1),
+            pltpu.VMEM((NY, SLAB, width), BF16),
+            pltpu.VMEM((NY - 1, SLAB, width), BF16),
+            pltpu.VMEM((2 * NX * line, 2 * DEAD), F32),
+            pltpu.VMEM((2 * NX * line, Q * DEAD), BF16),
+            pltpu.VMEM((2 * NX * line, Q * DEAD), BF16),
             pltpu.VMEM((2 * Q, DEAD, width), BF16),
             pltpu.VMEM((2 * Q, DEAD, width), BF16),
             pltpu.VMEM((2, 2, DEAD // 2, width), BF16),

time: 133 us -> 123 us (0.925)
  Pallas kernels: 128 us -> 118 us
    pallas_call x1, Pallas kernels: 128 us -> 118 us  [body(): pl.pallas_call(kernel, out_shape=(jax.ShapeDtypeStruct((DEAD, feats), BF1...]
where the time goes in v4:
time: 123 us
  Pallas kernels  118 us (96%)
  matrix products  4.16 us (3%)
    pallas_call x1, Pallas kernels, body(): pl.pallas_call(kernel, out_shape=(jax.ShapeDtypeStruct((DEAD, feats), BF1...  118 us
    dot_general x2, matrix products, dot_tn(): lax.dot_general(a, b, (((0,), (0,)), ((), ())), preferred_element_type=F32)  4.16 us

profile of v4, /device:TPU:1, one launch (start us, length us, event | category | flops | bytes accessed | tf_op | source)
XLA Modules:
  0.0 122.6 jit_solution(14787859386290333417)
XLA Ops:
  0.6 117.7 %shard_map.68 = (bf16[64,4608]{1,0:T(8,128)(2,1)}, bf16[64,4608]{1,0:T(8,128)(2,1)}, bf16[64,128]{1,0:T(8,128)(2,1)}) custom-call(bf16[3,4608]{1,0:T(4,128)(2,1)} %res_in.1, bf16[3,4608]{1,0:T(4,128)(2,1)} %err_in.1, bf16[4608,128]{1,0:T(8,128)(2,1)} %enc_in.1, bf16[128,4608]{1,0:T(8,128)(2,1)} %dec_in.1, s32[1,128]{1,0:T(1,128)} %bitcast.5), custom_call_target="tpu_custom_call" | custom-call | tf_op jit(solution)/shard_map/pallas_call | solution.py:434
  118.4 0.0 copy-start
  118.4 0.0 copy-start.1
  118.4 2.7 %convolution_convert_fusion.1 = bf16[4608,128]{1,0:T(8,128)(2,1)} fusion(bf16[64,4608]{1,0:T(8,128)(2,1)} %get-tuple-element.5, bf16[64,128]{1,0:T(8,128)(2,1)} %get-tuple-element.6), kind=kOutput, calls=%fused_computation.1 | convolution fusion | flops 76087296 | bytes 1785856 | tf_op jit(solution)/shard_map/dot_general | solution.py:29
  121.0 0.0 copy-done
  121.0 0.0 copy-done.1
  121.0 1.5 %convolution_convert_fusion = bf16[128,4608]{1,0:T(8,128)(2,1)} fusion(bf16[64,128]{1,0:T(8,128)(2,1)S(1)} %copy-done.1, bf16[64,4608]{1,0:T(8,128)(2,1)S(1)} %copy-done), kind=kOutput, calls=%fused_computation | convolution fusion | flops 76087296 | bytes 1785856 | tf_op jit(solution)/shard_map/dot_general | solution.py:29
Async XLA Ops:
  118.4 2.7 %copy-start = (bf16[64,4608]{1,0:T(8,128)(2,1)S(1)}, bf16[64,4608]{1,0:T(8,128)(2,1)}, u32[]{:S(2)}) copy-start(bf16[64,4608]{1,0:T(8,128)(2,1)} %get-tuple-element.7) | copy-start | bytes 1769476
  118.4 2.7 %copy-start.1 = (bf16[64,128]{1,0:T(8,128)(2,1)S(1)}, bf16[64,128]{1,0:T(8,128)(2,1)}, u32[]{:S(2)}) copy-start(bf16[64,128]{1,0:T(8,128)(2,1)} %get-tuple-element.6) | copy-start | bytes 49156

commit v5 on v4

--- a/solution.py
+++ b/solution.py
@@ -67,8 +67,8 @@
 def kernel(
     res_in, err_in, enc_in, dec_in, mask_in,
     dgrad_ref, egrad_ref, pick_ref,
-    e4, w4, ybuf, rbuf, gbuf, obuf, osib, s1, xrecv, s2, yrecv, ghost, aexp, pexp, zsend, zhalf, zrel, zrecv, zall,
-    res_ref, err_ref, enc_ref, dec_ref, mask_ref, l_s,
+    e4, w4, e4t, w4t, ybuf, rbuf, gbuf, obuf, osib, s1, xrecv, s2, yrecv, ghost, aexp, pexp, zsend, zhalf, zrel, zrecv, zall,
+    res_ref, err_ref, enc_ref, dec_ref, mask_ref, l_s, t_s,
     w_s, w_r, gy_s, gy_r, gx_s, gx_r, gs_s, gs_r, os_s, os_r, ox_s, ox_r, oy_s, oy_r,
     h_s, h_r, z_s, z_r, a_s, a_r, f_s, f_r,
 ):
@@ -144,7 +144,7 @@
         return copies
 
     def gather_x(buf, k, ycopies):
-        xcopies = []
+        xcopies, forward = [], []
         for h, cols in enumerate(chunks):
             for copy in ycopies[h]:
                 copy.wait_recv()
@@ -154,15 +154,13 @@
             xcopies.append(
                 {d: go(remote(mine, mine, gx_s.at[k, h, d - 1], gx_r.at[k, h, d - 1], xof(d))) for d in xorder}
             )
-        mine = buf.at[block(c, x)]
-        forward = {0: go(remote(mine, mine, gs_s.at[k, 0], gs_r.at[k, 0], sibling))}
+            forward.append({0: go(remote(mine, mine, gs_s.at[k, h, 0], gs_r.at[k, h, 0], sibling))})
         return xcopies, forward
 
-    def gather_next(buf, k, xcopies, forward, d):
-        for copies in xcopies:
-            copies[d].wait_recv()
-        got = buf.at[block(c, lax.rem(x + NX - d, NX))]
-        forward[d] = go(remote(got, got, gs_s.at[k, d], gs_r.at[k, d], sibling))
+    def gather_next(buf, k, xcopies, forward, d, h):
+        xcopies[h][d].wait_recv()
+        got = buf.at[block(c, lax.rem(x + NX - d, NX)), :, chunks[h]]
+        forward[h][d] = go(remote(got, got, gs_s.at[k, h, d], gs_r.at[k, h, d], sibling))
 
     loads[0].wait()
     ybuf[0, pl.ds(y, 1)] = to_slab(res_ref, width).astype(BF16)[None]
@@ -200,10 +198,13 @@
         weights[0].wait_recv()
         weights[1].wait_recv()
 
+    e4t[...] = e4[...].T
+    w4t[...] = w4[...].T
+
     def run_block(cc, xx):
         b = cc * NX + xx
         here = pl.ds(pl.multiple_of(b * line, 32 if line % 32 == 0 else 8), line)
-        pre = fold(dot_nt(rbuf[b], e4[...]))
+        pre = fold(dot_nn(rbuf[b], e4t[...]))
         val = jnp.exp(pre)
         ghost[here, :] = val
         spread = unfold(val)
@@ -226,9 +227,11 @@
     for i, d in enumerate(order):
         xx = lax.rem(x + NX - d, NX)
         if d:
-            gather_next(rbuf, 0, xcopies, forward, d)
+            for h in range(len(chunks)):
+                gather_next(rbuf, 0, xcopies, forward, d, h)
         run_block(c, xx)
-        forward[d].wait_recv()
+        for copies in forward:
+            copies[d].wait_recv()
         run_block(o, xx)
         ocopies[d] = go(remote(obuf.at[o * NX + xx], osib.at[xx], os_s.at[d], os_r.at[d], sibling))
         if i > 1:
@@ -262,13 +265,14 @@
     ybuf[1, pl.ds(y, 1)] = (scale * (scale * out - err) / err_rms).astype(BF16)[None]
     ycopies = gather_y(1)
     xcopies, forward = gather_x(gbuf, 1, ycopies)
-    for d in xorder:
-        gather_next(gbuf, 1, xcopies, forward, d)
-    for d in order:
-        forward[d].wait_recv()
+
+    def gather_chunk(h):
+        for d in xorder:
+            gather_next(gbuf, 1, xcopies, forward, d, h)
+        for d in order:
+            forward[h][d].wait_recv()
 
     tokens = 2 * plane * REAL
-    tile = min(width, 384)
     factor = 1.0 / math.sqrt(NZ * 2 * plane * 3)
     to_left = lax.rem(zhi + Q - 1, Q)
     to_right = lax.rem(zhi + 1, Q)
@@ -277,27 +281,26 @@
     top, low = pl.ds(0, DEAD // 2), pl.ds(DEAD // 2, DEAD // 2)
     half = Q // 2
 
-    def gradient(lhs, rhs, kind):
-        left = lhs[...]
-        for j in range(width // tile):
-            cols = pl.ds(j * tile, tile)
-            part = (dot_tn(left, rhs[:, :, cols].reshape(tokens, tile)) * factor).astype(BF16)
-            for q in range(Q):
-                zsend[kind * Q + q, :, cols] = part[q * DEAD : (q + 1) * DEAD]
-
-    def halves(kind):
-        return [
-            remote(
-                zsend.at[pl.ds(kind * Q + i * half, half)], zhalf.at[pl.ds(kind * Q + i * half, half)],
-                h_s.at[kind, i], h_r.at[kind, i], zof(d),
+    def halves(kind, h):
+        copies = []
+        for i, d in enumerate((1, NZ - 1)):
+            at_rows = pl.ds(kind * Q + i * half, half)
+            copies.append(
+                remote(
+                    zsend.at[at_rows, :, chunks[h]], zhalf.at[at_rows, :, chunks[h]],
+                    h_s.at[kind, h, i], h_r.at[kind, h, i], zof(d),
+                )
             )
-            for i, d in enumerate((1, NZ - 1))
-        ]
-
-    def send_halves(kind):
+        return copies
+
+    def gradient(lhs, rhs, kind, h):
+        part = (dot_tn(lhs[...], rhs[:, :, chunks[h]].reshape(tokens, -1)) * factor).astype(BF16)
+        for q in range(Q):
+            zsend[kind * Q + q, :, chunks[h]] = part[q * DEAD : (q + 1) * DEAD]
+
         @pl.when(jnp.logical_not(own))
         def _():
-            for copy in halves(kind):
+            for copy in halves(kind, h):
                 copy.start()
 
     def z_copy(kind, i):
@@ -326,9 +329,14 @@
         piece = zall.at[kind * Q + (zhi, to_left, to_right, across)[i]]
         return remote(piece, piece, f_s.at[kind, i], f_r.at[kind, i], sibling)
 
+    def store(kind, q):
+        cols = pl.ds(q * width, width)
+        return pltpu.make_async_copy(zall.at[kind * Q + q], (dgrad_ref, egrad_ref)[kind].at[:, cols], t_s.at[kind, q])
+
     def add_halves(kind):
-        for copy in halves(kind):
-            copy.wait_recv()
+        for h in range(len(chunks)):
+            for copy in halves(kind, h):
+                copy.wait_recv()
         for p, sends in ((across, (0, 1)), (to_right, (2,)), (to_left, (3,)), (zhi, ())):
             p = kind * Q + p
             zsend[p] = (zsend[p].astype(F32) + zhalf[p].astype(F32)).astype(BF16)
@@ -363,20 +371,23 @@
         for i in range(4, 6):
             a_copy(kind, i).wait_recv()
         hand(kind, 3).start()
-
-    gradient(aexp, gbuf, 0)
-    send_halves(0)
+        for q in range(Q):
+            store(kind, q).start()
+
+    for h in range(len(chunks)):
+        gather_chunk(h)
+        gradient(aexp, gbuf, 0, h)
     for b in range(2 * NX):
         here = pl.ds(b * line, line)
-        back = fold(dot_nt(gbuf[b], w4[...]))
+        back = fold(dot_nn(gbuf[b], w4t[...]))
         pexp[here, :] = unfold(back * ghost[here, :])
 
     @pl.when(own)
     def _():
         add_halves(0)
 
-    gradient(pexp, rbuf, 1)
-    send_halves(1)
+    for h in range(len(chunks)):
+        gradient(pexp, rbuf, 1, h)
 
     @pl.when(own)
     def _():
@@ -395,10 +406,12 @@
         for kind in range(2):
             for i in range(Q):
                 hand(kind, i).wait_recv()
-
-    for q in range(Q):
-        dgrad_ref[:, q * width : (q + 1) * width] = zall[q]
-        egrad_ref[:, q * width : (q + 1) * width] = zall[Q + q]
+            for q in range(Q):
+                store(kind, q).start()
+
+    for kind in range(2):
+        for q in range(Q):
+            store(kind, q).wait()
 
     @pl.when(own)
     def _():
@@ -414,8 +427,9 @@
     @pl.when(jnp.logical_not(own))
     def _():
         for kind in range(2):
-            for copy in halves(kind):
-                copy.wait_send()
+            for h in range(len(chunks)):
+                for copy in halves(kind, h):
+                    copy.wait_send()
 
     for copy in pending:
         copy.wait_send()
@@ -439,10 +453,12 @@
             jax.ShapeDtypeStruct((DEAD, 128), BF16),
         ),
         in_specs=[pl.BlockSpec(memory_space=pl.ANY)] * 5,
-        out_specs=(vmem,) * 3,
+        out_specs=(pl.BlockSpec(memory_space=pl.ANY),) * 2 + (vmem,),
         scratch_shapes=[
             pltpu.VMEM((Q * DEAD, width), BF16),
             pltpu.VMEM((Q * DEAD, width), BF16),
+            pltpu.VMEM((width, Q * DEAD), BF16),
+            pltpu.VMEM((width, Q * DEAD), BF16),
             pltpu.VMEM((2, NY, SLAB, width), BF16),
             held(2 * NX),
             held(2 * NX),
@@ -466,14 +482,15 @@
             pltpu.VMEM(dec_weight.shape, BF16),
             pltpu.VMEM((1, dead_mask.shape[0]), jnp.int32),
             dma((5,)),
+            dma((2, Q)),
             dma((2,)), dma((2,)),
             dma((2, 2, NY - 1)), dma((2, 2, NY - 1)),
             dma((2, 2, NX - 1)), dma((2, 2, NX - 1)),
-            dma((2, NX)), dma((2, NX)),
+            dma((2, 2, NX)), dma((2, 2, NX)),
             dma((NX,)), dma((NX,)),
             dma((NX - 1,)), dma((NX - 1,)),
             dma((NY - 1,)), dma((NY - 1,)),
-            dma((2, 2)), dma((2, 2)),
+            dma((2, 2, 2)), dma((2, 2, 2)),
             dma((2, 6)), dma((2, 6)),
             dma((2, 6)), dma((2, 6)),
             dma((2, Q)), dma((2, Q)),

time: 123 us -> 121 us (0.984)
  no operation moved by 1% of the time
where the time goes in v5:
time: 121 us
  Pallas kernels  117 us (97%)
  matrix products  4.16 us (3%)
    pallas_call x1, Pallas kernels, body(): pl.pallas_call(kernel, out_shape=(jax.ShapeDtypeStruct((DEAD, feats), BF1...  117 us
    dot_general x2, matrix products, dot_tn(): lax.dot_general(a, b, (((0,), (0,)), ((), ())), preferred_element_type=F32)  4.16 us

profile of v5, /device:TPU:1, one launch (start us, length us, event | category | flops | bytes accessed | tf_op | source)
XLA Modules:
  0.0 121.3 jit_solution(11929140275788463052)
XLA Ops:
  0.6 116.5 %shard_map.68 = (bf16[64,4608]{1,0:T(8,128)(2,1)}, bf16[64,4608]{1,0:T(8,128)(2,1)}, bf16[64,128]{1,0:T(8,128)(2,1)}) custom-call(bf16[3,4608]{1,0:T(4,128)(2,1)} %res_in.1, bf16[3,4608]{1,0:T(4,128)(2,1)} %err_in.1, bf16[4608,128]{1,0:T(8,128)(2,1)} %enc_in.1, bf16[128,4608]{1,0:T(8,128)(2,1)} %dec_in.1, s32[1,128]{1,0:T(1,128)} %bitcast.5), custom_call_target="tpu_custom_call" | custom-call | tf_op jit(solution)/shard_map/pallas_call | solution.py:448
  117.1 0.0 copy-start
  117.2 0.0 copy-start.1
  117.2 2.7 %convolution_convert_fusion.1 = bf16[4608,128]{1,0:T(8,128)(2,1)} fusion(bf16[64,4608]{1,0:T(8,128)(2,1)} %get-tuple-element.5, bf16[64,128]{1,0:T(8,128)(2,1)} %get-tuple-element.6), kind=kOutput, calls=%fused_computation.1 | convolution fusion | flops 76087296 | bytes 1785856 | tf_op jit(solution)/shard_map/dot_general | solution.py:29
  119.8 0.0 copy-done
  119.8 0.0 copy-done.1
  119.8 1.5 %convolution_convert_fusion = bf16[128,4608]{1,0:T(8,128)(2,1)} fusion(bf16[64,128]{1,0:T(8,128)(2,1)S(1)} %copy-done.1, bf16[64,4608]{1,0:T(8,128)(2,1)S(1)} %copy-done), kind=kOutput, calls=%fused_computation | convolution fusion | flops 76087296 | bytes 1785856 | tf_op jit(solution)/shard_map/dot_general | solution.py:29
Async XLA Ops:
  117.1 2.7 %copy-start = (bf16[64,4608]{1,0:T(8,128)(2,1)S(1)}, bf16[64,4608]{1,0:T(8,128)(2,1)}, u32[]{:S(2)}) copy-start(bf16[64,4608]{1,0:T(8,128)(2,1)} %get-tuple-element.7) | copy-start | bytes 1769476
  117.2 2.7 %copy-start.1 = (bf16[64,128]{1,0:T(8,128)(2,1)S(1)}, bf16[64,128]{1,0:T(8,128)(2,1)}, u32[]{:S(2)}) copy-start(bf16[64,128]{1,0:T(8,128)(2,1)} %get-tuple-element.6) | copy-start | bytes 49156

commit v6 on v5

--- a/solution.py
+++ b/solution.py
@@ -127,7 +127,7 @@
         pl.semaphore_signal(barrier, inc=1, device_id=dev, device_id_type=MESH)
     pl.semaphore_wait(barrier, len(partners))
 
-    cut = width // 256 * 128 + (128 if width % 256 else 0) if width > 128 else 128
+    cut = max(width // 256 * 128, 128)
     chunks = [pl.ds(0, cut)] + ([pl.ds(cut, width - cut)] if width > cut else [])
 
     line = NY * REAL

time: 121 us -> 121 us (level)
  no operation moved by 1% of the time
where the time goes in v6:
time: 121 us
  Pallas kernels  116 us (96%)
  matrix products  4.16 us (3%)
    pallas_call x1, Pallas kernels, body(): pl.pallas_call(kernel, out_shape=(jax.ShapeDtypeStruct((DEAD, feats), BF1...  116 us
    dot_general x2, matrix products, dot_tn(): lax.dot_general(a, b, (((0,), (0,)), ((), ())), preferred_element_type=F32)  4.16 us

profile of v6, /device:TPU:1, one launch (start us, length us, event | category | flops | bytes accessed | tf_op | source)
XLA Modules:
  0.0 120.8 jit_solution(605507241956154151)
XLA Ops:
  0.6 115.9 %shard_map.68 = (bf16[64,4608]{1,0:T(8,128)(2,1)}, bf16[64,4608]{1,0:T(8,128)(2,1)}, bf16[64,128]{1,0:T(8,128)(2,1)}) custom-call(bf16[3,4608]{1,0:T(4,128)(2,1)} %res_in.1, bf16[3,4608]{1,0:T(4,128)(2,1)} %err_in.1, bf16[4608,128]{1,0:T(8,128)(2,1)} %enc_in.1, bf16[128,4608]{1,0:T(8,128)(2,1)} %dec_in.1, s32[1,128]{1,0:T(1,128)} %bitcast.5), custom_call_target="tpu_custom_call" | custom-call | tf_op jit(solution)/shard_map/pallas_call | solution.py:448
  116.6 0.0 copy-start
  116.6 0.0 copy-start.1
  116.6 2.7 %convolution_convert_fusion.1 = bf16[4608,128]{1,0:T(8,128)(2,1)} fusion(bf16[64,4608]{1,0:T(8,128)(2,1)} %get-tuple-element.5, bf16[64,128]{1,0:T(8,128)(2,1)} %get-tuple-element.6), kind=kOutput, calls=%fused_computation.1 | convolution fusion | flops 76087296 | bytes 1785856 | tf_op jit(solution)/shard_map/dot_general | solution.py:29
  119.2 0.0 copy-done
  119.3 0.0 copy-done.1
  119.3 1.5 %convolution_convert_fusion = bf16[128,4608]{1,0:T(8,128)(2,1)} fusion(bf16[64,128]{1,0:T(8,128)(2,1)S(1)} %copy-done.1, bf16[64,4608]{1,0:T(8,128)(2,1)S(1)} %copy-done), kind=kOutput, calls=%fused_computation | convolution fusion | flops 76087296 | bytes 1785856 | tf_op jit(solution)/shard_map/dot_general | solution.py:29
Async XLA Ops:
  116.6 2.7 %copy-start = (bf16[64,4608]{1,0:T(8,128)(2,1)S(1)}, bf16[64,4608]{1,0:T(8,128)(2,1)}, u32[]{:S(2)}) copy-start(bf16[64,4608]{1,0:T(8,128)(2,1)} %get-tuple-element.7) | copy-start | bytes 1769476
  116.6 2.7 %copy-start.1 = (bf16[64,128]{1,0:T(8,128)(2,1)S(1)}, bf16[64,128]{1,0:T(8,128)(2,1)}, u32[]{:S(2)}) copy-start(bf16[64,128]{1,0:T(8,128)(2,1)} %get-tuple-element.6) | copy-start | bytes 49156
